TPU v7x, 128 devices: a whole 4x4x4 slice. The times are simulated.
128 devices in a mesh: blk: 16 (over x_lo, z, core), feat: 8 (over y, x_hi).
Axes of the slice: x: 4 (x_hi: 2, x_lo: 2; x = x_hi * 2 + x_lo), y: 4, z: 4, core: 2. Of those that a mesh axis runs over, the one named last changes fastest.
Arguments:
- node_feats: bfloat16 [65536, 1024], P(('blk', 'feat')), may hold values from -6 to 6
- weight: bfloat16 [1024, 1024], replicated, may hold values from -0.1875 to 0.1875
- bias_vec: float32 [1024], P('feat'), may hold values from -3 to 3
- block_vals: bfloat16 [512, 14, 128, 128], P('blk'), may hold values from -0.1875 to 0.1875
- block_cols: int32 [512, 14], P('blk'), may hold values from 0 to 511, as said below
- row_counts: int32 [512], P('blk'), may hold values from 2 to 14, as said below
- cotangent: bfloat16 [65536, 1024], P('blk', 'feat'), may hold values from -6 to 6
Outputs:
- hidden_out: bfloat16 [65536, 1024], P('blk', 'feat')
- grad_nodes: bfloat16 [65536, 1024], P(('blk', 'feat'))
- grad_weight: float32 [1024, 1024], P('blk', 'feat')
- grad_bias: float32 [1024], P('feat')
Inputs may be any that keep to these rules, and one draw needn't show every extreme that they name: `block_cols`: each block row names 14 different block columns. Groups are runs of 512 / 16 consecutive block rows; over all slots of one group's block rows, at most 22 different block columns belong to any one owning group (the group whose nodes they are), and this bound is reached. Only the first row_counts[r] slots of block row r are adjacency blocks; the other slots are ignored.
All inputs are finite; a program needn't handle non-finite values.
Results may differ from a plain program's by a relative error of at most 0.03.
The roundings to bfloat16 on the way count: a program that leaves them out, or rounds other values in their place, can miss the bound.
Values may be sent and summed in bfloat16 or wider, within the bound.
A program may use at most 192 MiB of HBM per device.

v0:
```python
import jax
import jax.numpy as jnp
from jax import lax
from jax.sharding import PartitionSpec as P


def local(node_feats, weight, bias_vec, block_vals, block_cols, row_counts, cotangent):
    col_width = bias_vec.shape[0]
    block_size = block_vals.shape[-1]
    slot_count = block_vals.shape[1]
    column_slot = lax.axis_index("feat") * col_width
    weight_cols = lax.dynamic_slice_in_dim(weight, column_slot, col_width, 1)
    node_rows = lax.all_gather(node_feats, "feat", axis=0, tiled=True)
    mapped = jnp.dot(node_rows, weight_cols, preferred_element_type=jnp.float32).astype(
        jnp.bfloat16
    )
    flat_cols = block_cols.reshape(-1)
    slot_ids = jnp.arange(slot_count, dtype=jnp.int32)
    alive = slot_ids[None, :] < row_counts[:, None]
    everything = lax.all_gather(mapped, "blk", axis=0, tiled=True)
    stacked = everything.reshape(-1, block_size, col_width)
    picked = stacked[block_cols] * alive[:, :, None, None].astype(jnp.bfloat16)
    summed = jnp.einsum("rkij,rkjc->ric", block_vals, picked, preferred_element_type=jnp.float32)
    pre_act = summed.reshape(-1, col_width) + bias_vec[None, :]
    hidden_out = jnp.maximum(pre_act, 0.0).astype(jnp.bfloat16)
    grad_pre = jnp.where(pre_act > 0.0, cotangent.astype(jnp.float32), 0.0).astype(jnp.bfloat16)
    grad_blocks = grad_pre.reshape(-1, block_size, col_width)
    contrib = jnp.einsum(
        "rkij,ric->rkjc", block_vals, grad_blocks, preferred_element_type=jnp.float32
    )
    contrib = (contrib * alive[:, :, None, None].astype(jnp.float32)).reshape(
        -1, block_size, col_width
    )
    row_count = grad_pre.shape[0] * lax.axis_size("blk")
    block_total = row_count // block_size
    target_ids = flat_cols
    inside = (target_ids >= 0) & (target_ids < block_total)
    target_ids = jnp.where(inside, target_ids, block_total)
    landed = jax.ops.segment_sum(contrib, target_ids, num_segments=block_total + 1)
    grad_mid = lax.psum_scatter(
        landed[:block_total].reshape(row_count, col_width).astype(jnp.bfloat16),
        "blk",
        scatter_dimension=0,
        tiled=True,
    )
    grad_panel = lax.all_to_all(grad_mid, "feat", split_axis=0, concat_axis=1, tiled=True)
    grad_nodes = lax.dot_general(
        grad_panel, weight, (((1,), (1,)), ((), ())), preferred_element_type=jnp.float32
    ).astype(jnp.bfloat16)
    partial_cols = lax.dot_general(
        node_rows, grad_mid, (((0,), (0,)), ((), ())), preferred_element_type=jnp.float32
    )
    grad_weight = lax.psum_scatter(
        partial_cols.astype(jnp.bfloat16), "blk", scatter_dimension=0, tiled=True
    ).astype(jnp.float32)
    grad_bias = lax.psum(jnp.sum(grad_pre.astype(jnp.float32), axis=0), "blk")
    return (hidden_out, grad_nodes, grad_weight, grad_bias)


def solution(mesh):
    in_specs = (
        P(("blk", "feat"), None),
        P(),
        P("feat"),
        P("blk", None, None, None),
        P("blk", None),
        P("blk"),
        P("blk", "feat"),
    )
    out_specs = (P("blk", "feat"), P(("blk", "feat"), None), P("blk", "feat"), P("feat"))
    return jax.shard_map(local, mesh=mesh, in_specs=in_specs, out_specs=out_specs, check_vma=False)
```

profile of v0, /device:TPU:0, one launch (start us, length us, event | category | flops | bytes accessed | tf_op | source)
XLA Modules:
  0.0 622.3 jit_solution(6093675081834503718)
XLA Ops:
  7.2 0.0 all-gather.3.cloned.1.call-start
  7.2 0.7 all-gather.3.cloned.1.call-update
  7.9 0.0 all-gather.5.cloned.1.call-start
  8.0 111.9 %all-gather.3.cloned.1.call-done = bf16[4096,1024]{1,0:T(8,128)(2,1)} async-done(((bf16[512,1024]{1,0:T(8,128)(2,1)}), bf16[4096,1024]{1,0:T(8,128)(2,1)}) %all-gather.3.cloned.1.call-update) | async-done | bytes 8388624 | tf_op jit(solution)/shard_map/all_gather | solution.py:13
  119.8 7.3 %fusion.3 = bf16[4096,128]{0,1:T(8,128)(2,1)} fusion(bf16[4096,1024]{1,0:T(8,128)(2,1)} %all-gather.3.cloned.1.call-done, bf16[1024,1024]{1,0:T(8,128)(2,1)S(1)} %copy-done, s32[]{:T(128)S(6)} %select_n.21), kind=kOutput, calls=%fused_computation.8 | convolution fusion | flops 1074266112 | bytes 9699332 | tf_op jit(solution)/shard_map/dot_general | solution.py:14
  127.1 0.2 reduce-scatter.5.cloned.1.call-start
  127.4 0.8 copy.29
  128.1 0.7 compare_select_fusion
  128.8 0.1 copy.27
  128.9 0.1 reshape.109
  129.0 0.1 reshape.104
  129.2 0.7 fusion.6
  129.9 86.9 %all-gather.5.cloned.1.call-done = bf16[65536,128]{0,1:T(8,128)(2,1)} async-done(((bf16[4096,128]{0,1:T(8,128)(2,1)}), bf16[65536,128]{0,1:T(8,128)(2,1)}) %all-gather.5.cloned.1.call-update) | async-done | bytes 16777232 | tf_op jit(solution)/shard_map/all_gather | solution.py:20
  216.8 22.4 %copy.36 = bf16[65536,128]{1,0:T(8,128)(2,1)} copy(bf16[65536,128]{0,1:T(8,128)(2,1)} %all-gather.5.cloned.1.call-done) | data formatting | bytes 33554432 | tf_op jit(solution)/shard_map/reshape | solution.py:21
  239.2 19.2 %gather_fusion = bf16[448,128,128]{2,1,0:T(8,128)(2,1)} fusion(bf16[512,128,128]{2,1,0:T(8,128)(2,1)} %bitcast.42, s32[1024]{0:T(1024)S(1)} %pad_clamp_fusion), kind=kCustom, calls=%fused_computation | custom fusion | bytes 29361920 | tf_op jit(solution)/shard_map/gather | solution.py:22
  258.4 11.6 %fusion = f32[32,128,128,1]{1,2,3,0:T(8,128)S(1)} fusion(bf16[32,14,128,128]{3,2,1,0:T(8,128)(2,1)} %param.10, bf16[32,14,128,128]{3,2,1,0:T(8,128)(2,1)} %bitcast.43, bf16[32,14]{1,0:T(8,128)(2,1)S(1)} %get-tuple-element.24), kind=kOutput, calls=%fused_computation.4 | convolution fusion | flops 1908408320 | bytes 31458176 | tf_op jit(solution)/shard_map/rkij,rkjc->ric/dot_general | solution.py:23
  270.0 1.5 convert_reduce_fusion
  271.5 14.8 %broadcast_multiply_fusion = f32[32,128,14,128]{3,1,2,0:T(8,128)} fusion(f32[32,14]{1,0:T(8,128)S(1)} %get-tuple-element.23, bf16[32,128,128,1]{2,1,3,0:T(8,128)(2,1)S(1)} %bitcast.45, bf16[32,14,128,128]{3,2,1,0:T(8,128)(2,1)} %param.10), kind=kOutput, calls=%fused_computation.3 | convolution fusion | flops 1886388224 | bytes 45090560 | tf_op jit(solution)/shard_map/rkij,ric->rkjc/dot_general | solution.py:28
  286.3 29.5 %copy.31 = f32[448,128,128]{2,1,0:T(8,128)} copy(f32[448,128,128]{1,2,0:T(8,128)} %bitcast.40) | data formatting | bytes 58720256 | tf_op jit(solution)/shard_map/reshape | solution.py:31
  315.9 11.1 %broadcast_in_dim.8 = f32[513,128,128]{2,1,0:T(8,128)} broadcast(f32[]{:T(128)} %constant.11.clone.1), dimensions={} | broadcast | bytes 33619972 | tf_op jit(solution)/shard_map/broadcast_in_dim | solution.py:39
  327.0 92.9 %scatter_fusion = f32[513,128,128]{2,1,0:T(8,128)} fusion(f32[513,128,128]{2,1,0:T(8,128)} %broadcast_in_dim.8, s32[448]{0:T(512)S(1)} %bitcast.48, f32[448,128,128]{2,1,0:T(8,128)} %copy.31), kind=kCustom, calls=%fused_computation.1 | custom fusion | flops 7340032 | bytes 88082176 | tf_op jit(solution)/shard_map/scatter-add | solution.py:39
  419.8 17.7 %slice.9 = bf16[512,128,128]{2,1,0:T(8,128)(2,1)} slice(f32[513,128,128]{2,1,0:T(8,128)} %scatter_fusion), slice={[0:512], [0:128], [0:128]} | slice | bytes 33554432 | tf_op jit(solution)/shard_map/slice | solution.py:41
  437.6 99.9 %reduce-scatter.5.cloned.1.call-done = bf16[4096,128]{1,0:T(8,128)(2,1)} async-done(((bf16[65536,128]{1,0:T(8,128)(2,1)}), bf16[4096,128]{1,0:T(8,128)(2,1)}) %reduce-scatter.5.cloned.1.call-update) | async-done | bytes 1048592 | tf_op jit(solution)/shard_map/reduce_scatter | solution.py:40
  537.4 6.4 %all-to-all-start = ((bf16[8,512,128]{2,1,0:T(8,128)(2,1)}), bf16[8,512,128]{2,1,0:T(8,128)(2,1)S(1)}, u32[]{:S(2)}, u32[]{:S(2)}) async-start(bf16[8,512,128]{2,1,0:T(8,128)(2,1)} %bitcast.44), calls=%async_computation.1 | async-start | bytes 2097152 | tf_op jit(solution)/shard_map/all_to_all | solution.py:46
  543.9 5.0 fusion.4
  548.9 0.8 copy.39
  549.7 29.6 %psum.7 = f32[128]{0:T(128)} all-reduce(f32[128]{0:T(128)S(1)} %get-tuple-element.20), channel_id=1, replica_groups=mesh['blk'=16,'feat'=8] {'blk'}, use_global_device_ids=true, to_apply=%region_4.5 | all-reduce | flops 128 | bytes 1024 | tf_op jit(solution)/shard_map/psum | solution.py:56
  579.3 30.1 %reduce-scatter.7.cloned.1.call-done = bf16[64,128]{1,0:T(8,128)(2,1)} async-done(((bf16[1024,128]{1,0:T(8,128)(2,1)}), bf16[64,128]{1,0:T(8,128)(2,1)}) %reduce-scatter.7.cloned.1.call-update) | async-done | bytes 16400
  609.4 0.8 copy.40
  610.3 0.7 copy.33
  611.0 1.3 copy.32
  612.3 3.5 convolution_convert_fusion.1
  (13 shorter events, 0.1 us)
Async XLA Ops:
  7.2 112.7 %copy-start = (bf16[1024,1024]{1,0:T(8,128)(2,1)S(1)}, bf16[1024,1024]{1,0:T(8,128)(2,1)}, u32[]{:S(2)}) copy-start(bf16[1024,1024]{1,0:T(8,128)(2,1)} %param.8) | copy-start | bytes 6291460
  7.2 112.7 %all-gather.3.cloned.1.call-start = ((), (), s32[]{:S(2)}) async-start(), calls=%async_computation.3 | async-start | bytes 9437184 | tf_op jit(solution)/shard_map/all_gather | solution.py:13
  7.9 208.9 %all-gather.5.cloned.1.call-start = ((), (), s32[]{:S(2)}) async-start(), calls=%async_computation.4 | async-start | bytes 17825792 | tf_op jit(solution)/shard_map/all_gather | solution.py:20
  127.1 410.3 %reduce-scatter.5.cloned.1.call-start = ((), (), s32[]{:S(2)}) async-start(), calls=%async_computation.5 | async-start | bytes 17825792 | tf_op jit(solution)/shard_map/reduce_scatter | solution.py:40
  258.3 11.7 %copy-start.1 = (bf16[4096,128]{1,0:T(8,128)(2,1)S(1)}, bf16[4096,128]{1,0:T(8,128)(2,1)}, u32[]{:S(2)}) copy-start(bf16[4096,128]{1,0:T(8,128)(2,1)} %param.13) | copy-start | bytes 3145732
  258.4 11.7 %copy-start.2 = (f32[128]{0:T(128)S(1)}, f32[128]{0:T(128)}, u32[]{:S(2)}) copy-start(f32[128]{0:T(128)} %param.9) | copy-start | bytes 1540
  537.4 73.6 %all-to-all-start = ((bf16[8,512,128]{2,1,0:T(8,128)(2,1)}), bf16[8,512,128]{2,1,0:T(8,128)(2,1)S(1)}, u32[]{:S(2)}, u32[]{:S(2)}) async-start(bf16[8,512,128]{2,1,0:T(8,128)(2,1)} %bitcast.44), calls=%async_computation.1 | async-start | bytes 2097152 | tf_op jit(solution)/shard_map/all_to_all | solution.py:46
  543.8 65.6 %reduce-scatter.7.cloned.1.call-start = ((), (), s32[]{:S(2)}) async-start(), calls=%async_computation.6 | async-start | bytes 278528
Sparse Core Ops, SparseCore 0:
  10.4 109.4 all-gather.2
  127.2 89.5 all-gather.4
  437.7 99.7 reduce-scatter.4
  549.9 59.5 reduce-scatter.6
where the time goes:
time: 625 us; the launch traced here: 622 us
  waiting for transfers between devices  330 us (53%)
  local copies, waits for them, and re-layouts  105 us (17%)
  other arithmetic  95.8 us (15%)
  matrix products  42.2 us (7%)
  blocking collectives  29.6 us (5%)
  between operations  13.8 us (2%)
  starting transfers between devices  6.73 us (1%)
    all_gather x1, waiting for transfers between devices, local(): node_rows = lax.all_gather(node_feats, 'feat', axis=0, tiled=True)  112 us
    reduce_scatter x1, waiting for transfers between devices, local(): lax.psum_scatter(landed[:block_total].reshape(row_count, col_width).astyp...  99.9 us
    scatter-add x1, other arithmetic, local(): jax.ops.segment_sum(contrib, target_ids, num_segments=block_total + 1)  92.9 us
    all_gather x1, waiting for transfers between devices, local(): everything = lax.all_gather(mapped, 'blk', axis=0, tiled=True)  86.9 us
    unnamed x5, waiting for transfers between devices  30.9 us
    psum x1, blocking collectives, local(): grad_bias = lax.psum(jnp.sum(grad_pre.astype(jnp.float32), axis=0), 'blk')  29.6 us
    reshape x1, local copies, waits for them, and re-layouts, local(): (contrib * alive[:, :, None, None].astype(jnp.float32)).reshape(-1, block...  29.5 us
    reshape x1, local copies, waits for them, and re-layouts, local(): stacked = everything.reshape(-1, block_size, col_width)  22.4 us
  transfers between devices with their start and end apart: 5, of which 4 were waited for; matrix products, arithmetic and copies ran while one was open for 2% of the time, Pallas kernels for 0%

commit v1 on v0

v1 whole, which is shorter than its diff:
```python
import jax
import jax.numpy as jnp
from jax import lax
from jax.experimental import pallas as pl
from jax.experimental.pallas import tpu as pltpu
from jax.sharding import PartitionSpec as P

MESH = pl.DeviceIdType.MESH
BF = jnp.bfloat16
F32 = jnp.float32
N_FEAT = 8
N_GRP = 16
ROWS = 512
COL = 128
BS = 128
KMAX = 14
PER = 32
VMEM_BYTES = 56 * 2**20
OWN, PX, NP, NM, PA, PB, FC, FD = range(8)


def place():
    b = lax.axis_index("blk")
    f = lax.axis_index("feat")
    xl = lax.div(b, 8)
    z = lax.rem(lax.div(b, 2), 4)
    c = lax.rem(b, 2)
    return xl, z, c, f


def grp(xl, z, c):
    return xl * 8 + z * 2 + c


def zadd(z, d):
    return lax.rem(z + d, 4)


def units(xl, z, c):
    o = 1 - xl
    return (
        grp(xl, z, c),
        grp(o, z, c),
        grp(xl, zadd(z, 1), c),
        grp(xl, zadd(z, 3), c),
        grp(o, zadd(z, 1), c),
        grp(o, zadd(z, 3), c),
        grp(xl, zadd(z, 2), c),
        grp(o, zadd(z, 2), c),
    )


def rcopy(src, dst, ssem, rsem, dev):
    return pltpu.make_async_remote_copy(
        src_ref=src, dst_ref=dst, send_sem=ssem, recv_sem=rsem, device_id=dev, device_id_type=MESH
    )


def greet(peers):
    bar = pltpu.get_barrier_semaphore()
    for dev in peers:
        pl.semaphore_signal(bar, inc=1, device_id=dev, device_id_type=MESH)
    pl.semaphore_wait(bar, len(peers))


def each(lo, hi, body):
    def step(i, carry):
        body(i)
        return carry

    lax.fori_loop(lo, hi, step, 0)


def gather_kernel(x_ref, w_ref, t_ref, tr, a_send, a_recv, o_send, f_send, s_send, recv, s_recv, l_sem):
    xl, z, c, f = place()
    u = units(xl, z, c)
    g = u[OWN]
    dx = {"blk": u[PX], "feat": f}
    dzp = {"blk": u[NP], "feat": f}
    dzm = {"blk": u[NM], "feat": f}
    ds = {"blk": grp(xl, z, 1 - c), "feat": f}
    greet([dx, dzp, dzm, ds] + [{"blk": g, "feat": lax.rem(f + i, N_FEAT)} for i in range(1, N_FEAT)])

    def chunk(i):
        return lax.rem(f + N_FEAT - i, N_FEAT)

    def product(i):
        to = lax.rem(f + i, N_FEAT)
        cols = pl.ds(pl.multiple_of(to * COL, COL), COL)
        tr[i] = jnp.dot(x_ref[...], w_ref[:, cols], preferred_element_type=F32).astype(BF)
        return to

    def a2a(i, to):
        return rcopy(tr.at[i], t_ref.at[g, f], a_send.at[i], a_recv.at[i], {"blk": g, "feat": to})

    def send_first(i):
        to = product(i)
        a2a(i, to).start()

    each(1, N_FEAT, send_first)
    product(0)
    mine = pltpu.make_async_copy(tr.at[0], t_ref.at[g, f], l_sem)
    mine.start()
    mine.wait()

    def own_copy(k, i, dev, r):
        p = t_ref.at[g, chunk(i)]
        return rcopy(p, p, o_send.at[k, i], recv.at[r, i], dev)

    def sib_copy(k, i):
        p = t_ref.at[u[k], chunk(i)]
        return rcopy(p, p, s_send.at[k, i], s_recv.at[k, i], ds)

    def fwd(k, i, slot, dev, r):
        p = t_ref.at[u[k], chunk(i)]
        return rcopy(p, p, f_send.at[slot, lax.rem(i, 4)], recv.at[r, i], dev)

    def arrived(k, i):
        p = t_ref.at[u[k], chunk(i)]
        rcopy(p, p, l_sem, recv.at[k, i], dx).wait_recv()

    def own_all(i):
        own_copy(0, i, dx, PX).start()
        own_copy(1, i, dzp, NM).start()
        own_copy(2, i, dzm, NP).start()
        sib_copy(OWN, i).start()

    own_all(0)

    def own_next(i):
        p = t_ref.at[g, chunk(i)]
        rcopy(p, p, l_sem, a_recv.at[i], dx).wait_recv()
        own_all(i)

    each(1, N_FEAT, own_next)

    def low(i):
        arrived(PX, i)
        fwd(PX, i, 0, dzm, PA).start()
        sib_copy(PX, i).start()
        arrived(NP, i)
        fwd(NP, i, 1, dzm, FC).start()
        sib_copy(NP, i).start()
        arrived(NM, i)
        fwd(NM, i, 2, dx, PB).start()
        sib_copy(NM, i).start()

    def high(i):
        arrived(PX, i)
        fwd(PX, i, 3, dzp, PB).start()
        sib_copy(PX, i).start()
        arrived(NM, i)
        fwd(NM, i, 4, dzp, FC).start()
        sib_copy(NM, i).start()
        arrived(NP, i)
        fwd(NP, i, 5, dx, PA).start()
        sib_copy(NP, i).start()

    each(0, 4, low)
    each(4, 8, high)

    def last(i):
        arrived(PA, i)
        fwd(PA, i, 6, dzm, FD).start()
        sib_copy(PA, i).start()
        arrived(PB, i + 4)
        fwd(PB, i + 4, 7, dzp, FD).start()
        sib_copy(PB, i + 4).start()

    each(0, 4, last)

    def rest(i):
        arrived(PA, i + 4)
        sib_copy(PA, i + 4).start()
        arrived(PB, i)
        sib_copy(PB, i).start()
        arrived(FC, i)
        sib_copy(FC, i).start()
        arrived(FC, i + 4)
        sib_copy(FC, i + 4).start()

    each(0, 4, rest)

    def far(i):
        arrived(FD, i)
        sib_copy(FD, i).start()

    each(0, 8, far)

    def finish(i):
        own_copy(0, i, dx, PX).wait_send()
        own_copy(1, i, dzp, NM).wait_send()
        own_copy(2, i, dzm, NP).wait_send()
        for k in range(8):
            sib_copy(k, i).wait_send()
            p = t_ref.at[u[k], chunk(i)]
            rcopy(p, p, l_sem, s_recv.at[k, i], ds).wait_recv()

    each(0, 8, finish)

    def finish_fwd(i):
        for slot, k in enumerate((PX, NP, NM, PX, NM, NP, PA, PB)):
            p = t_ref.at[u[k], chunk(i)]
            rcopy(p, p, f_send.at[slot, i], recv.at[0, i], dx).wait_send()

    each(0, 4, finish_fwd)

    def finish_a2a(i):
        a2a(i, lax.rem(f + i, N_FEAT)).wait_send()

    each(1, N_FEAT, finish_a2a)


def gather_call(x, w):
    dma = pltpu.SemaphoreType.DMA
    return pl.pallas_call(
        gather_kernel,
        out_shape=jax.ShapeDtypeStruct((N_GRP, N_FEAT, ROWS, COL), BF),
        in_specs=[pl.BlockSpec(memory_space=pltpu.VMEM)] * 2,
        out_specs=pl.BlockSpec(memory_space=pltpu.HBM),
        scratch_shapes=[
            pltpu.VMEM((N_FEAT, ROWS, COL), BF),
            dma((8,)),
            dma((8,)),
            dma((3, 8)),
            dma((8, 4)),
            dma((8, 8)),
            dma((8, 8)),
            dma((8, 8)),
            dma,
        ],
        compiler_params=pltpu.CompilerParams(
            collective_id=0, has_side_effects=True, vmem_limit_bytes=VMEM_BYTES
        ),
        name="gather",
    )(x, w)


def block_kernel(cols, cnt, v_ref, cot_ref, bias_ref, t_ref, hid_ref, q_ref, bsum_ref, tbuf, acc, qbuf, seen, tsem, qsem):
    r = pl.program_id(0)

    def fetch(row, slot, k):
        return pltpu.make_async_copy(t_ref.at[cols[row, k]], tbuf.at[slot, k], tsem.at[slot, k])

    @pl.when(r == 0)
    def _():
        def clear(i):
            seen[i] = 0

        each(0, N_GRP * PER, clear)
        bsum_ref[...] = jnp.zeros_like(bsum_ref)
        for k in range(KMAX):
            fetch(0, 0, k).start()

    slot = lax.rem(r, 2)

    @pl.when(r + 1 < PER)
    def _():
        for k in range(KMAX):
            fetch(r + 1, 1 - slot, k).start()

    for k in range(KMAX):
        fetch(r, slot, k).wait()

    n = cnt[r]

    def pair(p):
        a = jnp.where(2 * p < n, v_ref[0, 2 * p], jnp.zeros((BS, BS), BF))
        b = jnp.where(2 * p + 1 < n, v_ref[0, 2 * p + 1], jnp.zeros((BS, BS), BF))
        return jnp.concatenate([a, b], axis=1)

    pre = jnp.zeros((BS, COL), F32)
    for p in range(KMAX // 2):
        rhs = tbuf[slot, 2 * p : 2 * p + 2].reshape(2 * BS, COL)
        pre = pre + jnp.dot(pair(p), rhs, preferred_element_type=F32)
    pre = pre + bias_ref[...]
    hid_ref[...] = jnp.maximum(pre, 0.0).astype(BF)
    grad = jnp.where(pre > 0.0, cot_ref[...].astype(F32), 0.0)
    bsum_ref[...] += jnp.sum(grad.reshape(BS // 8, 8, COL), axis=0)
    grad_t = grad.T.astype(BF)
    prods = []
    for p in range(KMAX // 2):
        prods.append(jnp.dot(grad_t, pair(p), preferred_element_type=F32))
    for k in range(KMAX):
        col = cols[r, k]
        live = k < n
        old = seen[col]
        seen[col] = jnp.where(live, 1, old)
        part = prods[k // 2][:, (k % 2) * BS : (k % 2 + 1) * BS]

        @pl.when(live & (old == 0))
        def _():
            acc[col] = part

        @pl.when(live & (old != 0))
        def _():
            acc[col] += part

    @pl.when(r == PER - 1)
    def _():
        def out_copy(i):
            return pltpu.make_async_copy(qbuf.at[lax.rem(i, 2)], q_ref.at[i], qsem.at[lax.rem(i, 2)])

        def group(i):
            @pl.when(i >= 2)
            def _():
                out_copy(i - 2).wait()

            def block(j):
                b = i * PER + j
                qbuf[lax.rem(i, 2), j] = jnp.where(seen[b] != 0, acc[b], 0.0).astype(BF)

            each(0, PER, block)
            out_copy(i).start()

        each(0, N_GRP, group)
        out_copy(N_GRP - 2).wait()
        out_copy(N_GRP - 1).wait()


def block_call(cols, cnt, vals, cot, bias, t):
    rows = PER * BS
    return pl.pallas_call(
        block_kernel,
        out_shape=(
            jax.ShapeDtypeStruct((rows, COL), BF),
            jax.ShapeDtypeStruct((N_GRP, PER, BS, BS), BF),
            jax.ShapeDtypeStruct((8, COL), F32),
        ),
        grid_spec=pltpu.PrefetchScalarGridSpec(
            num_scalar_prefetch=2,
            grid=(PER,),
            in_specs=[
                pl.BlockSpec((1, KMAX, BS, BS), lambda r, *_: (r, 0, 0, 0)),
                pl.BlockSpec((BS, COL), lambda r, *_: (r, 0)),
                pl.BlockSpec((1, COL), lambda r, *_: (0, 0)),
                pl.BlockSpec(memory_space=pltpu.HBM),
            ],
            out_specs=[
                pl.BlockSpec((BS, COL), lambda r, *_: (r, 0)),
                pl.BlockSpec(memory_space=pltpu.HBM),
                pl.BlockSpec((8, COL), lambda r, *_: (0, 0)),
            ],
            scratch_shapes=[
                pltpu.VMEM((2, KMAX, BS, COL), BF),
                pltpu.VMEM((N_GRP * PER, BS, BS), F32),
                pltpu.VMEM((2, PER, BS, BS), BF),
                pltpu.SMEM((N_GRP * PER,), jnp.int32),
                pltpu.SemaphoreType.DMA((2, KMAX)),
                pltpu.SemaphoreType.DMA((2,)),
            ],
        ),
        compiler_params=pltpu.CompilerParams(vmem_limit_bytes=VMEM_BYTES),
        name="blocks",
    )(cols, cnt, vals, cot, bias, t)


def scatter_kernel(
    q_ref, bsum_ref, x_ref, w_ref, gn_ref, gw_ref, gb_ref,
    own, sib, zp, zm, xp, zp_o, zm_o, x_o, gmo, gm, xt, gwp, gwsib, gws, gwr, gw2, gw2r, bsib, bpl,
    own_sem, sib_send, sib_recv, d_send, d_recv, o_send, o_recv, m_send, m_recv,
    ws_send, ws_recv, wf_send, wf_recv, wp_send, wp_recv, b_send, b_recv, l_sem,
):
    xl, z, c, f = place()
    u = units(xl, z, c)
    v = units(xl, z, 1 - c)
    g = u[OWN]
    q = xl * 4 + z
    dx = {"blk": u[PX], "feat": f}
    dzp = {"blk": u[NP], "feat": f}
    dzm = {"blk": u[NM], "feat": f}
    ds = {"blk": v[OWN], "feat": f}

    def feat_dev(i):
        return {"blk": g, "feat": lax.rem(f + i, N_FEAT)}

    def plane_dev(i):
        return {"blk": lax.rem(q + i, 8) * 2 + c, "feat": f}

    greet([ds] + [feat_dev(i) for i in range(1, 8)] + [plane_dev(i) for i in range(1, 8)])

    bs_copy = rcopy(bsum_ref, bsib, b_send.at[0], b_recv.at[0], ds)
    bs_copy.start()

    order = (FD, PA, PB, FC, PX, NP, NM, OWN)

    def mine_copy(k):
        return pltpu.make_async_copy(q_ref.at[u[k]], own.at[k], own_sem.at[k])

    def sib_copy(k):
        return rcopy(q_ref.at[v[k]], sib.at[k], sib_send.at[k], sib_recv.at[k], ds)

    def begin(k):
        mine_copy(k).start()
        sib_copy(k).start()

    def have(k):
        mine_copy(k).wait()
        sib_copy(k).wait()

    def chunk(i):
        return lax.rem(f + N_FEAT - 1 - i, N_FEAT)

    def total(k, i, *more):
        ch = chunk(i)
        s = own[k, ch].astype(F32) + sib[k, ch].astype(F32)
        for m in more:
            s = s + m.astype(F32)
        return s

    def ship(slot, j, k, i, dst, dev):
        return rcopy(own.at[k, chunk(i)], dst, d_send.at[slot, j], d_recv.at[slot, j], dev)

    def ship_o(slot, k, i, dst, dev):
        return rcopy(own.at[k, chunk(i)], dst, o_send.at[slot, i], o_recv.at[slot, i], dev)

    def put(k, i, value):
        own[k, chunk(i)] = value.astype(BF)

    def got(slot, j):
        ship(slot, j, 0, 0, zp.at[0, j], dx).wait_recv()

    begin(FD)
    begin(PA)
    have(FD)
    begin(PB)

    def send_d(j):
        put(FD, j, total(FD, j))
        ship(0, j, FD, j, zp.at[0, j], dzp).start()
        put(FD, j + 4, total(FD, j + 4))
        ship(1, j, FD, j + 4, zm.at[0, j], dzm).start()

    each(0, 4, send_d)
    have(PA)
    begin(FC)

    def send_a(j):
        put(PA, j + 4, total(PA, j + 4))
        ship(2, j, PA, j + 4, xp.at[0, j], dx).start()

    each(0, 4, send_a)
    have(PB)
    begin(PX)

    def send_b(j):
        put(PB, j, total(PB, j))
        ship(3, j, PB, j, xp.at[1, j], dx).start()

    each(0, 4, send_b)
    have(FC)
    begin(NP)

    def send_c(j):
        put(FC, j, total(FC, j))
        ship(4, j, FC, j, zp.at[2, j], dzp).start()
        put(FC, j + 4, total(FC, j + 4))
        ship(5, j, FC, j + 4, zm.at[2, j], dzm).start()

    each(0, 4, send_c)
    have(PX)
    begin(NM)

    def send_ab(j):
        got(0, j)
        put(PA, j, total(PA, j, zp[0, j]))
        ship(6, j, PA, j, zp.at[1, j], dzp).start()
        got(1, j)
        put(PB, j + 4, total(PB, j + 4, zm[0, j]))
        ship(7, j, PB, j + 4, zm.at[1, j], dzm).start()

    each(0, 4, send_ab)
    have(NP)
    begin(OWN)
    have(NM)

    for a in range(8):
        for b in range(4):
            xt[a * 128 : (a + 1) * 128, b * 128 : (b + 1) * 128] = (
                x_ref[b * 128 : (b + 1) * 128, a * 128 : (a + 1) * 128].astype(F32).T.astype(BF)
            )
    bs_copy.wait()
    bpl[q] = bsum_ref[...] + bsib[...]

    def b_copy(i):
        return rcopy(bpl.at[q], bpl.at[q], b_send.at[i], b_recv.at[i], plane_dev(i))

    each(1, 8, lambda i: b_copy(i).start())

    def send_n_low(j):
        got(4, j)
        put(NP, j, total(NP, j, zp[2, j]))
        ship_o(0, NP, j, zp_o.at[j], dzp).start()
        got(3, j)
        put(NM, j, total(NM, j, xp[1, j]))
        ship_o(1, NM, j, zm_o.at[j], dzm).start()

    each(0, 4, send_n_low)

    def send_p(j):
        got(6, j)
        put(PX, j, total(PX, j, zp[1, j]))
        ship_o(2, PX, j, x_o.at[j], dx).start()

    each(0, 4, send_p)

    def send_n_high(j):
        i = j + 4
        got(2, j)
        put(NP, i, total(NP, i, xp[0, j]))
        ship_o(0, NP, i, zp_o.at[i], dzp).start()
        got(5, j)
        put(NM, i, total(NM, i, zm[2, j]))
        ship_o(1, NM, i, zm_o.at[i], dzm).start()
        got(7, j)
        put(PX, i, total(PX, i, zm[1, j]))
        ship_o(2, PX, i, x_o.at[i], dx).start()

    each(0, 4, send_n_high)
    have(OWN)

    def m_copy(i):
        cols = pl.ds(pl.multiple_of(f * COL, COL), COL)
        return rcopy(gmo.at[i], gm.at[:, cols], m_send.at[i], m_recv.at[i], {"blk": g, "feat": chunk(i)})

    def own_part(i):
        for slot, dst in enumerate((zp_o, zm_o, x_o)):
            rcopy(own.at[NP, 0], dst.at[i], l_sem, o_recv.at[slot, i], dx).wait_recv()
        s = total(OWN, i, zp_o[i], zm_o[i], x_o[i])
        for b in range(4):
            gmo[i, b * BS : (b + 1) * BS, :] = s[b * BS : (b + 1) * BS].T.astype(BF)

    def own_send(i):
        own_part(i)
        m_copy(i).start()

    each(0, 7, own_send)
    own_part(7)
    here = pltpu.make_async_copy(gmo.at[7], gm.at[:, pl.ds(pl.multiple_of(f * COL, COL), COL)], l_sem)
    here.start()
    here.wait()
    each(0, 7, lambda i: m_copy(i).wait())

    for j in range(4):
        part = jnp.dot(xt[...], gm[:, j * 256 : (j + 1) * 256], preferred_element_type=F32).astype(BF)
        gwp[2 * j] = part[:, :128].reshape(8, 2, 64, 128)
        gwp[2 * j + 1] = part[:, 128:].reshape(8, 2, 64, 128)
    ws = rcopy(gwp.at[:, :, 1 - c], gwsib, ws_send, ws_recv, ds)
    ws.start()
    for j in range(2):
        gn_ref[:, j * 256 : (j + 1) * 256] = lax.dot_general(
            gm[...], w_ref[j * 256 : (j + 1) * 256, :], (((1,), (1,)), ((), ())), preferred_element_type=F32
        ).astype(BF)
    ws.wait()

    def wf_copy(i):
        return rcopy(gws.at[lax.rem(f + i, N_FEAT)], gwr.at[i], wf_send.at[i], wf_recv.at[i], feat_dev(i))

    def wf_sum(i):
        to = lax.rem(f + i, N_FEAT)
        gws[to] = (gwp[to, :, c].astype(F32) + gwsib[to].astype(F32)).astype(BF)

    def wf_step(i):
        wf_sum(i)
        wf_copy(i).start()

    each(1, 8, wf_step)
    wf_sum(0)
    for j in range(2, 4):
        gn_ref[:, j * 256 : (j + 1) * 256] = lax.dot_general(
            gm[...], w_ref[j * 256 : (j + 1) * 256, :], (((1,), (1,)), ((), ())), preferred_element_type=F32
        ).astype(BF)
    each(1, 8, lambda i: b_copy(i).wait())
    gb_ref[...] = jnp.sum(jnp.sum(bpl[...], axis=0), axis=0, keepdims=True)
    each(1, 8, lambda i: wf_copy(i).wait())

    def wp_copy(i):
        return rcopy(gw2.at[lax.rem(q + i, 8)], gw2r.at[i], wp_send.at[i], wp_recv.at[i], plane_dev(i))

    def wp_sum(i):
        to = lax.rem(q + i, 8)
        s = gws[f, to].astype(F32)
        for k in range(1, 8):
            s = s + gwr[k, to].astype(F32)
        return to, s

    def wp_step(i):
        to, s = wp_sum(i)
        gw2[to] = s.astype(BF)
        wp_copy(i).start()

    each(1, 8, wp_step)
    s = wp_sum(0)[1]
    each(1, 8, lambda i: wp_copy(i).wait())
    for k in range(1, 8):
        s = s + gw2r[k].astype(F32)
    gw_ref[...] = s

    def finish(j):
        for slot in range(8):
            ship(slot, j, 0, 0, zp.at[0, j], dx).wait_send()

    each(0, 4, finish)

    def finish_o(i):
        for slot, dst in enumerate((zp_o, zm_o, x_o)):
            ship_o(slot, NP, i, dst.at[i], dx).wait_send()

    each(0, 8, finish_o)


def scatter_call(q, bsum, x, w):
    dma = pltpu.SemaphoreType.DMA
    unit = (8, ROWS, COL)
    vm = pltpu.VMEM
    spec = pl.BlockSpec(memory_space=pltpu.VMEM)
    return pl.pallas_call(
        scatter_kernel,
        out_shape=(
            jax.ShapeDtypeStruct((ROWS, N_FEAT * COL), BF),
            jax.ShapeDtypeStruct((64, COL), F32),
            jax.ShapeDtypeStruct((1, COL), F32),
        ),
        in_specs=[pl.BlockSpec(memory_space=pltpu.HBM), spec, spec, spec],
        out_specs=(spec, spec, spec),
        scratch_shapes=[
            vm((8,) + unit, BF),
            vm((8,) + unit, BF),
            vm((3, 4, ROWS, COL), BF),
            vm((3, 4, ROWS, COL), BF),
            vm((2, 4, ROWS, COL), BF),
            vm(unit, BF),
            vm(unit, BF),
            vm(unit, BF),
            vm(unit, BF),
            vm((ROWS, N_FEAT * COL), BF),
            vm((N_FEAT * COL, ROWS), BF),
            vm((8, 8, 2, 64, 128), BF),
            vm((8, 8, 64, 128), BF),
            vm((8, 8, 64, 128), BF),
            vm((8, 8, 64, 128), BF),
            vm((8, 64, 128), BF),
            vm((8, 64, 128), BF),
            vm((8, COL), F32),
            vm((8, 8, COL), F32),
            dma((8,)),
            dma((8,)),
            dma((8,)),
            dma((8, 4)),
            dma((8, 4)),
            dma((3, 8)),
            dma((3, 8)),
            dma((8,)),
            dma((8,)),
            dma,
            dma,
            dma((8,)),
            dma((8,)),
            dma((8,)),
            dma((8,)),
            dma((8,)),
            dma((8,)),
            dma,
        ],
        compiler_params=pltpu.CompilerParams(
            collective_id=1, has_side_effects=True, vmem_limit_bytes=VMEM_BYTES
        ),
        name="scatter",
    )(q, bsum, x, w)


def local(node_feats, weight, bias_vec, block_vals, block_cols, row_counts, cotangent):
    t = gather_call(node_feats, weight).reshape(N_GRP * PER, BS, COL)
    hidden, q, bsum = block_call(
        block_cols, row_counts, block_vals, cotangent, bias_vec.reshape(1, COL), t
    )
    gn, gw, gb = scatter_call(q.reshape(N_GRP, N_FEAT, ROWS, COL), bsum, node_feats, weight)
    return hidden, gn, gw, gb.reshape(COL)


def solution(mesh):
    in_specs = (
        P(("blk", "feat"), None),
        P(),
        P("feat"),
        P("blk", None, None, None),
        P("blk", None),
        P("blk"),
        P("blk", "feat"),
    )
    out_specs = (P("blk", "feat"), P(("blk", "feat"), None), P("blk", "feat"), P("feat"))
    return jax.shard_map(local, mesh=mesh, in_specs=in_specs, out_specs=out_specs, check_vma=False)
```

time: 625 us -> 233 us (0.37)
  waiting for transfers between devices: 330 us -> 0 us
  Pallas kernels: 0 us -> 224 us
  local copies, waits for them, and re-layouts: 105 us -> 6.19 us
  other arithmetic: 95.8 us -> 0 us
  matrix products: 42.2 us -> 0 us
  blocking collectives: 29.6 us -> 0 us
  between operations: 13.8 us -> 0.66 us
  starting transfers between devices: 6.73 us -> 0 us
    pallas_call x0 -> x3, Pallas kernels: none -> 224 us  [the longest x1 96.7 us: scatter_call(): pl.pallas_call(scatter_kernel, out_shape=(jax.ShapeDtypeStruct((ROWS, N_F...]
    all_gather x2 -> x0, waiting for transfers between devices: 199 us -> none  [the longest x1 112 us: local(): node_rows = lax.all_gather(node_feats, 'feat', axis=0, tiled=True)]
    reduce_scatter x1 -> x0, waiting for transfers between devices: 99.9 us -> none  [local(): lax.psum_scatter(landed[:block_total].reshape(row_count, col_width).astyp...]
    scatter-add x1 -> x0, other arithmetic: 92.9 us -> none  [local(): jax.ops.segment_sum(contrib, target_ids, num_segments=block_total + 1)]
    reshape x3 -> x0, local copies, waits for them, and re-layouts: 52 us -> none  [the longest x1 29.5 us: local(): (contrib * alive[:, :, None, None].astype(jnp.float32)).reshape(-1, block...]
    dot_general x5 -> x0, matrix products: 42.2 us -> none  [the longest x1 14.8 us: local(): jnp.einsum('rkij,ric->rkjc', block_vals, grad_blocks, preferred_element_t...]
    unnamed x5 -> x0, waiting for transfers between devices: 30.9 us -> none
    psum x1 -> x0, blocking collectives: 29.6 us -> none  [local(): grad_bias = lax.psum(jnp.sum(grad_pre.astype(jnp.float32), axis=0), 'blk')]
  transfers between devices with their start and end apart: 5 -> 0, of which waited for: 4 -> 0; matrix products, arithmetic and copies ran while one was open for 2% -> 0% of each run, Pallas kernels for 0% -> 0%
where the time goes in v1:
time: 233 us; the launch traced here: 231 us
  Pallas kernels  224 us (96%)
  local copies, waits for them, and re-layouts  6.19 us (3%)
    pallas_call x1, Pallas kernels, scatter_call(): pl.pallas_call(scatter_kernel, out_shape=(jax.ShapeDtypeStruct((ROWS, N_F...  96.7 us
    pallas_call x1, Pallas kernels, gather_call(): pl.pallas_call(gather_kernel, out_shape=jax.ShapeDtypeStruct((N_GRP, N_FE...  77.7 us
    pallas_call x1, Pallas kernels, block_call(): pl.pallas_call(block_kernel, out_shape=(jax.ShapeDtypeStruct((rows, COL),...  49.5 us
    unnamed x4, local copies, waits for them, and re-layouts  6.19 us

profile of v1, /device:TPU:0, one launch (start us, length us, event | category | flops | bytes accessed | tf_op | source)
XLA Modules:
  0.0 230.7 jit_solution(18028489677939794546)
XLA Ops:
  0.6 1.4 copy.11.cols
  2.0 77.7 %gather.1 = bf16[16,8,512,128]{3,2,1,0:T(8,128)(2,1)} custom-call(bf16[512,1024]{1,0:T(8,128)(2,1)} %x_ref.3, bf16[1024,1024]{1,0:T(8,128)(2,1)} %w_ref.3), custom_call_target="tpu_custom_call" | custom-call | tf_op jit(solution)/shard_map/gather/pallas_call | solution.py:216
  79.7 49.5 %blocks.1 = (bf16[4096,128]{1,0:T(8,128)(2,1)}, bf16[16,32,128,128]{3,2,1,0:T(8,128)(2,1)}, f32[8,128]{1,0:T(8,128)}) custom-call(s32[32,14]{1,0:T(8,128)} %copy.11.cols, s32[32]{0:T(128)} %cnt.1, bf16[32,14,128,128]{3,2,1,0:T(8,128)(2,1)} %v_ref.1, bf16[4096,128]{1,0:T(8,128)(2,1)} %cot_ref.1, f32[1,128]{1,0:T(1,128)} %bitcast.6, bf16[512,128,128]{2,1,0:T(8,128)(2,1)} %bitcast.4), custom_call_target="tpu_custom_call" | custom-call | tf_op jit(solution)/shard_map/blocks/pallas_call | solution.py:323
  129.2 96.7 %scatter.1 = (bf16[512,1024]{1,0:T(8,128)(2,1)}, f32[64,128]{1,0:T(8,128)}, f32[1,128]{1,0:T(1,128)}) custom-call(bf16[16,8,512,128]{3,2,1,0:T(8,128)(2,1)} %bitcast.5, f32[8,128]{1,0:T(8,128)} %get-tuple-element.12.bsum_ref, bf16[512,1024]{1,0:T(8,128)(2,1)} %x_ref.3, bf16[1024,1024]{1,0:T(8,128)(2,1)} %w_ref.3), custom_call_target="tpu_custom_call" | custom-call | tf_op jit(solution)/shard_map/scatter/pallas_call | solution.py:617
  225.9 2.3 copy.15
  228.2 1.4 copy.16
  229.5 1.2 copy.17
